TPU v7x, 32 devices: a whole 2x2x4 slice. The times are simulated.
32 devices in a mesh: fsdp: 2 (over y), context: 4 (over x, core), tensor: 4 (over z).
Axes of the slice: x: 2, y: 2, z: 4, core: 2. Of those that a mesh axis runs over, the one named last changes fastest.
Arguments:
- tokens: bfloat16 [16, 2048, 960], P('fsdp', ('context', 'tensor')), may hold values from -6 to 6
- gain_attn: bfloat16 [960], P(('fsdp', 'context')), may hold values from 0.5 to 1.5
- w_query: bfloat16 [960, 960], P(('fsdp', 'context')), may hold values from -0.25 to 0.25
- w_key: bfloat16 [960, 320], P(('fsdp', 'context')), may hold values from -0.25 to 0.25
- w_value: bfloat16 [960, 320], P(('fsdp', 'context')), may hold values from -0.1875 to 0.1875
- w_out: bfloat16 [960, 960], P(None, ('fsdp', 'context')), may hold values from -1.25 to 1.25
- gain_mlp: bfloat16 [960], P(('fsdp', 'context')), may hold values from 0.5 to 1.5
- w_gate: bfloat16 [960, 2560], P(('fsdp', 'context'), 'tensor'), may hold values from -0.1875 to 0.1875
- w_up: bfloat16 [960, 2560], P(('fsdp', 'context'), 'tensor'), may hold values from -0.1875 to 0.1875
- w_down: bfloat16 [2560, 960], P('tensor', ('fsdp', 'context')), may hold values from -0.25 to 0.25
- cotangent: bfloat16 [16, 2048, 960], P('fsdp', ('context', 'tensor')), may hold values from -6 to 6
Outputs:
- output: float32 [16, 2048, 960], P('fsdp', ('context', 'tensor'))
- grad_tokens: float32 [16, 2048, 960], P('fsdp', ('context', 'tensor'))
- grad_gain_attn: float32 [960], P(('fsdp', 'context'))
- grad_query: float32 [960, 960], P(('fsdp', 'context'))
- grad_key: float32 [960, 320], P(('fsdp', 'context'))
- grad_value: float32 [960, 320], P(('fsdp', 'context'))
- grad_out: float32 [960, 960], P(None, ('fsdp', 'context'))
- grad_gain_mlp: float32 [960], P(('fsdp', 'context'))
- grad_gate: float32 [960, 2560], P(('fsdp', 'context'), 'tensor')
- grad_up: float32 [960, 2560], P(('fsdp', 'context'), 'tensor')
- grad_down: float32 [2560, 960], P('tensor', ('fsdp', 'context'))
All inputs are finite; a program needn't handle non-finite values.
Results may differ from a plain program's by a relative error of at most 0.018.
Values may be sent and summed in bfloat16 or wider, within the bound.
A program may use at most 256 MiB of HBM per device.

v0:
```python
import math

import jax
import jax.numpy as jnp
from jax import lax
from jax.sharding import PartitionSpec as P

HEADS = 15
KV_HEADS = 5
HEAD_DIM = 64


epsilon = 1e-05
rope_base = 10000.0
neg_large = -1e30
key_block = 256


def rms_scale(values):
    return lax.rsqrt(jnp.mean(values * values, axis=-1, keepdims=True) + epsilon)


def tables(positions):
    step_index = jnp.arange(HEAD_DIM // 2).astype(jnp.float32)
    frequency = jnp.power(rope_base, -2.0 * step_index / HEAD_DIM)
    angles = positions.astype(jnp.float32)[:, None] * frequency[None, :]
    return (jnp.cos(angles), jnp.sin(angles))


def rotate(values, cos_t, sin_t):
    half_dim = values.shape[-1] // 2
    first_half = values[..., :half_dim]
    second_half = values[..., half_dim:]
    return jnp.concatenate(
        [first_half * cos_t - second_half * sin_t, second_half * cos_t + first_half * sin_t],
        axis=-1,
    )


def contract_rows(left_mat, right_mat):
    return lax.dot_general(
        left_mat, right_mat, (((0,), (0,)), ((), ())), preferred_element_type=jnp.float32
    )


def contract_cols(left_mat, right_mat):
    return lax.dot_general(
        left_mat, right_mat, (((1,), (1,)), ((), ())), preferred_element_type=jnp.float32
    )


def body(
    tokens, gain_attn, w_query, w_key, w_value, w_out, gain_mlp, w_gate, w_up, w_down, cotangent
):
    gathered = (
        lax.all_gather(gain_attn, ("fsdp", "context"), axis=0, tiled=True),
        lax.all_gather(w_query, ("fsdp", "context"), axis=0, tiled=True),
        lax.all_gather(w_key, ("fsdp", "context"), axis=0, tiled=True),
        lax.all_gather(w_value, ("fsdp", "context"), axis=0, tiled=True),
        lax.all_gather(w_out, ("fsdp", "context"), axis=1, tiled=True),
        lax.all_gather(gain_mlp, ("fsdp", "context"), axis=0, tiled=True),
        lax.all_gather(w_gate, ("fsdp", "context"), axis=0, tiled=True),
        lax.all_gather(w_up, ("fsdp", "context"), axis=0, tiled=True),
        lax.all_gather(w_down, ("fsdp", "context"), axis=1, tiled=True),
    )
    g_attn = gathered[0].astype(jnp.float32)
    w_query_all, w_key_all, w_value_all, w_out_all = (
        gathered[1],
        gathered[2],
        gathered[3],
        gathered[4],
    )
    g_mlp = gathered[5].astype(jnp.float32)
    w_gate_all, w_up_all, w_down_all = (gathered[6], gathered[7], gathered[8])
    seq_count, row_count, model_width = tokens.shape
    group_size = HEADS // KV_HEADS
    kv_width = KV_HEADS * HEAD_DIM
    q_width = HEADS * HEAD_DIM
    inv_root = 1.0 / math.sqrt(HEAD_DIM)
    seq_devices = lax.axis_size(("context", "tensor"))
    positions = lax.axis_index(("context", "tensor")) * row_count + jnp.arange(row_count)
    last_pos = positions[row_count - 1]
    cos_t, sin_t = tables(positions)
    cos_b = cos_t[:, None, :]
    sin_b = sin_t[:, None, :]
    inputs = tokens.astype(jnp.float32)
    rms_attn = rms_scale(inputs)
    normed_attn = (inputs * rms_attn * g_attn).astype(jnp.bfloat16)
    flat_attn = normed_attn.reshape(-1, model_width)
    query_lin = jnp.dot(flat_attn, w_query_all, preferred_element_type=jnp.float32).reshape(
        seq_count, row_count, HEADS, HEAD_DIM
    )
    key_lin = jnp.dot(flat_attn, w_key_all, preferred_element_type=jnp.float32).reshape(
        seq_count, row_count, KV_HEADS, HEAD_DIM
    )
    value_lin = jnp.dot(flat_attn, w_value_all, preferred_element_type=jnp.float32).reshape(
        seq_count, row_count, kv_width
    )
    queries = rotate(query_lin, cos_b, sin_b).astype(jnp.bfloat16)
    key_rot = rotate(key_lin, cos_b, sin_b).astype(jnp.bfloat16)
    key_value = jnp.concatenate(
        [key_rot.reshape(seq_count, row_count, kv_width), value_lin.astype(jnp.bfloat16)], axis=-1
    )
    query_grouped = queries.reshape(seq_count, row_count, KV_HEADS, group_size, HEAD_DIM)

    def split_block(shard_rows, block_start, block_len):
        block_rows = lax.dynamic_slice_in_dim(shard_rows, block_start, block_len, 1)
        key_part = block_rows[..., :kv_width].reshape(seq_count, block_len, KV_HEADS, HEAD_DIM)
        value_part = block_rows[..., kv_width:].reshape(seq_count, block_len, KV_HEADS, HEAD_DIM)
        return (key_part, value_part)

    def visible_blocks(block_len, block_total):
        return jnp.clip(last_pos // block_len + 1, 0, block_total)

    stat_shape = (seq_count, KV_HEADS, group_size, row_count)
    init_state = (
        jnp.full(stat_shape, neg_large, jnp.float32),
        jnp.zeros(stat_shape, jnp.float32),
        jnp.zeros(stat_shape + (HEAD_DIM,), jnp.float32),
    )
    shard_rows = lax.all_gather(key_value, ("context", "tensor"), axis=1, tiled=True)
    total_keys = shard_rows.shape[1]
    block_len = math.gcd(total_keys, key_block)

    def one_block(block_index, loop_state):
        top_run, sum_run, acc_run = loop_state
        block_start = block_index * block_len
        key_part, value_part = split_block(shard_rows, block_start, block_len)
        scores = (
            jnp.einsum(
                "sqhgd,skhd->shgqk", query_grouped, key_part, preferred_element_type=jnp.float32
            )
            * inv_root
        )
        allowed = (block_start + jnp.arange(block_len))[None, :] <= positions[:, None]
        scores = jnp.where(allowed, scores, neg_large)
        top_new = jnp.maximum(top_run, jnp.max(scores, axis=-1))
        expo_part = jnp.where(allowed, jnp.exp(scores - top_new[..., None]), 0.0)
        shrink = jnp.exp(top_run - top_new)
        sum_new = sum_run * shrink + jnp.sum(expo_part, axis=-1)
        acc_new = acc_run * shrink[..., None] + jnp.einsum(
            "shgqk,skhd->shgqd",
            expo_part.astype(jnp.bfloat16),
            value_part,
            preferred_element_type=jnp.float32,
        )
        return (top_new, sum_new, acc_new)

    upper = visible_blocks(block_len, total_keys // block_len)
    top_all, sum_all, acc_all = lax.fori_loop(0, upper, one_block, init_state)
    log_sum = top_all + jnp.log(sum_all)
    heads_grouped = jnp.transpose(acc_all / sum_all[..., None], (0, 3, 1, 2, 4))
    heads_out = heads_grouped.reshape(seq_count, row_count, q_width).astype(jnp.bfloat16)
    flat_heads = heads_out.reshape(-1, q_width)
    branch = jnp.dot(flat_heads, w_out_all, preferred_element_type=jnp.float32).reshape(
        seq_count, row_count, model_width
    )
    middle = inputs + branch
    rms_mlp = rms_scale(middle)
    normed_mlp = (middle * rms_mlp * g_mlp).astype(jnp.bfloat16)
    w_gate_use, w_up_use, w_down_use = (
        lax.all_gather(w_gate_all, "tensor", axis=1, tiled=True),
        lax.all_gather(w_up_all, "tensor", axis=1, tiled=True),
        lax.all_gather(w_down_all, "tensor", axis=0, tiled=True),
    )
    flat_mlp = normed_mlp.reshape(-1, model_width)
    gate_pre = jnp.dot(flat_mlp, w_gate_use, preferred_element_type=jnp.float32)
    up_pre = jnp.dot(flat_mlp, w_up_use, preferred_element_type=jnp.float32)
    sigma_gate = jax.nn.sigmoid(gate_pre)
    silu_gate = gate_pre * sigma_gate
    hidden = (silu_gate * up_pre).astype(jnp.bfloat16)
    partial_out = jnp.dot(hidden, w_down_use, preferred_element_type=jnp.float32)
    mlp_out = partial_out.reshape(seq_count, row_count, model_width)
    result = middle + mlp_out
    flat_grad = cotangent.reshape(-1, model_width)
    d_hidden = contract_cols(flat_grad, w_down_use)
    d_gate = (d_hidden * up_pre * sigma_gate * (1.0 + gate_pre * (1.0 - sigma_gate))).astype(
        jnp.bfloat16
    )
    d_up = (d_hidden * silu_gate).astype(jnp.bfloat16)
    grad_down_part = contract_rows(hidden, flat_grad)
    grad_gate_part = contract_rows(flat_mlp, d_gate)
    grad_up_part = contract_rows(flat_mlp, d_up)
    d_normed = contract_cols(d_gate, w_gate_use) + contract_cols(d_up, w_up_use)
    d_normed = d_normed.reshape(seq_count, row_count, model_width)
    grad_gate_part, grad_up_part, grad_down_part = (
        lax.psum_scatter(grad_gate_part, "tensor", scatter_dimension=1, tiled=True),
        lax.psum_scatter(grad_up_part, "tensor", scatter_dimension=1, tiled=True),
        lax.psum_scatter(grad_down_part, "tensor", scatter_dimension=0, tiled=True),
    )
    norm_mid = middle * rms_mlp
    scaled_mid = d_normed * g_mlp
    gain_mlp_part = jnp.sum(d_normed * norm_mid, axis=(0, 1))
    d_middle = cotangent.astype(jnp.float32) + rms_mlp * (
        scaled_mid - norm_mid * jnp.mean(scaled_mid * norm_mid, axis=-1, keepdims=True)
    )
    d_branch = d_middle.astype(jnp.bfloat16).reshape(-1, model_width)
    out_part = contract_rows(flat_heads, d_branch)
    d_heads = contract_cols(d_branch, w_out_all).astype(jnp.bfloat16)
    d_heads_g = d_heads.reshape(seq_count, row_count, KV_HEADS, group_size, HEAD_DIM)
    row_delta = jnp.transpose(
        jnp.sum(d_heads_g.astype(jnp.float32) * heads_grouped, axis=-1), (0, 2, 3, 1)
    )
    kv_buffer = jnp.zeros((seq_count, row_count * seq_devices, 2 * kv_width), jnp.float32)
    back_init = (jnp.zeros(stat_shape + (HEAD_DIM,), jnp.float32), kv_buffer)
    attend_shard_rows = lax.all_gather(key_value, ("context", "tensor"), axis=1, tiled=True)
    total_keys = attend_shard_rows.shape[1]
    attend_block_len = math.gcd(total_keys, key_block)

    def one_block(block_index, loop_state):
        dq_acc, dkv_acc = loop_state
        block_start = block_index * attend_block_len
        key_part, value_part = split_block(attend_shard_rows, block_start, attend_block_len)
        scores = (
            jnp.einsum(
                "sqhgd,skhd->shgqk", query_grouped, key_part, preferred_element_type=jnp.float32
            )
            * inv_root
        )
        allowed = (block_start + jnp.arange(attend_block_len))[None, :] <= positions[:, None]
        prob_part = jnp.where(allowed, jnp.exp(scores - log_sum[..., None]), 0.0)
        d_probs = jnp.einsum(
            "sqhgd,skhd->shgqk", d_heads_g, value_part, preferred_element_type=jnp.float32
        )
        d_scores = (prob_part * (d_probs - row_delta[..., None])).astype(jnp.bfloat16)
        dq_acc = dq_acc + jnp.einsum(
            "shgqk,skhd->shgqd", d_scores, key_part, preferred_element_type=jnp.float32
        )
        d_key = (
            jnp.einsum(
                "shgqk,sqhgd->skhd", d_scores, query_grouped, preferred_element_type=jnp.float32
            )
            * inv_root
        )
        d_value = jnp.einsum(
            "shgqk,sqhgd->skhd",
            prob_part.astype(jnp.bfloat16),
            d_heads_g,
            preferred_element_type=jnp.float32,
        )
        update = jnp.concatenate(
            [
                d_key.reshape(seq_count, attend_block_len, kv_width),
                d_value.reshape(seq_count, attend_block_len, kv_width),
            ],
            axis=-1,
        )
        current = lax.dynamic_slice_in_dim(dkv_acc, block_start, attend_block_len, 1)
        dkv_acc = lax.dynamic_update_slice_in_dim(dkv_acc, current + update, block_start, 1)
        return (dq_acc, dkv_acc)

    upper = visible_blocks(attend_block_len, total_keys // attend_block_len)
    dq_all, dkv_all = lax.fori_loop(0, upper, one_block, back_init)
    dkv_own = lax.psum_scatter(dkv_all, ("context", "tensor"), scatter_dimension=1, tiled=True)
    d_query = jnp.transpose(dq_all * inv_root, (0, 3, 1, 2, 4)).reshape(
        seq_count, row_count, HEADS, HEAD_DIM
    )
    d_query_lin = rotate(d_query, cos_b, -sin_b).astype(jnp.bfloat16).reshape(-1, q_width)
    d_key_rot = dkv_own[..., :kv_width].reshape(seq_count, row_count, KV_HEADS, HEAD_DIM)
    d_key_lin = rotate(d_key_rot, cos_b, -sin_b).astype(jnp.bfloat16).reshape(-1, kv_width)
    d_value_lin = dkv_own[..., kv_width:].astype(jnp.bfloat16).reshape(-1, kv_width)
    query_part = contract_rows(flat_attn, d_query_lin)
    key_grad_part = contract_rows(flat_attn, d_key_lin)
    value_grad_part = contract_rows(flat_attn, d_value_lin)
    d_normed_attn = (
        contract_cols(d_query_lin, w_query_all)
        + contract_cols(d_key_lin, w_key_all)
        + contract_cols(d_value_lin, w_value_all)
    )
    d_normed_attn = d_normed_attn.reshape(seq_count, row_count, model_width)
    norm_in = inputs * rms_attn
    scaled_in = d_normed_attn * g_attn
    gain_attn_part = jnp.sum(d_normed_attn * norm_in, axis=(0, 1))
    grad_tokens = d_middle + rms_attn * (
        scaled_in - norm_in * jnp.mean(scaled_in * norm_in, axis=-1, keepdims=True)
    )
    shards = (
        lax.psum_scatter(gain_attn_part, ("fsdp", "context"), scatter_dimension=0, tiled=True),
        lax.psum_scatter(query_part, ("fsdp", "context"), scatter_dimension=0, tiled=True),
        lax.psum_scatter(key_grad_part, ("fsdp", "context"), scatter_dimension=0, tiled=True),
        lax.psum_scatter(value_grad_part, ("fsdp", "context"), scatter_dimension=0, tiled=True),
        lax.psum_scatter(out_part, ("fsdp", "context"), scatter_dimension=1, tiled=True),
        lax.psum_scatter(gain_mlp_part, ("fsdp", "context"), scatter_dimension=0, tiled=True),
        lax.psum_scatter(grad_gate_part, ("fsdp", "context"), scatter_dimension=0, tiled=True),
        lax.psum_scatter(grad_up_part, ("fsdp", "context"), scatter_dimension=0, tiled=True),
        lax.psum_scatter(grad_down_part, ("fsdp", "context"), scatter_dimension=1, tiled=True),
    )
    replicated = lax.psum(
        (shards[0], shards[1], shards[2], shards[3], shards[4], shards[5]), "tensor"
    )
    return (
        result,
        grad_tokens,
        replicated[0],
        replicated[1],
        replicated[2],
        replicated[3],
        replicated[4],
        replicated[5],
        shards[6],
        shards[7],
        shards[8],
    )


def solution(mesh):
    placed = (
        P("fsdp", ("context", "tensor"), None),
        P(("fsdp", "context")),
        P(("fsdp", "context"), None),
        P(("fsdp", "context"), None),
        P(("fsdp", "context"), None),
        P(None, ("fsdp", "context")),
        P(("fsdp", "context")),
        P(("fsdp", "context"), "tensor"),
        P(("fsdp", "context"), "tensor"),
        P("tensor", ("fsdp", "context")),
        P("fsdp", ("context", "tensor"), None),
    )
    return jax.shard_map(
        body,
        mesh=mesh,
        in_specs=placed,
        out_specs=(
            P("fsdp", ("context", "tensor"), None),
            P("fsdp", ("context", "tensor"), None),
            P(("fsdp", "context")),
            P(("fsdp", "context"), None),
            P(("fsdp", "context"), None),
            P(("fsdp", "context"), None),
            P(None, ("fsdp", "context")),
            P(("fsdp", "context")),
            P(("fsdp", "context"), "tensor"),
            P(("fsdp", "context"), "tensor"),
            P("tensor", ("fsdp", "context")),
        ),
        check_vma=False,
    )
```

profile of v0, /device:TPU:0, one launch (start us, length us, event | category | flops | bytes accessed | tf_op | source)
XLA Modules:
  0.0 2260.6 jit_solution(3566972014727607047)
XLA Ops:
  13.7 15.2 all-reduce.13
  29.0 10.3 all-gather
  67.5 22.9 %all-gather.26.cloned.1.call-done = bf16[640,960]{0,1:T(8,128)(2,1)} async-done(((bf16[640,120]{0,1:T(8,128)(2,1)}), bf16[640,960]{0,1:T(8,128)(2,1)}) %all-gather.26.cloned.1.call-update) | async-done | bytes 1228816 | tf_op jit(solution)/shard_map/all_gather | solution.py:64
  90.5 29.0 %all-gather.14.cloned.1.call-done = bf16[960,960]{1,0:T(8,128)(2,1)} async-done(((bf16[120,960]{1,0:T(8,128)(2,1)}), bf16[960,960]{1,0:T(8,128)(2,1)}) %all-gather.14.cloned.1.call-update) | async-done | bytes 1843216 | tf_op jit(solution)/shard_map/all_gather | solution.py:57
  128.1 108.7 %all-gather.12.cloned.1.call-done = bf16[8,2048,640]{1,2,0:T(8,128)(2,1)} async-done(((bf16[8,128,640]{1,2,0:T(8,128)(2,1)}), bf16[8,2048,640]{1,2,0:T(8,128)(2,1)}) %all-gather.12.cloned.1.call-update) | async-done | bytes 20971536 | tf_op jit(solution)/shard_map/all_gather | solution.py:121
  239.2 29.0 %while.28 = (s32[]{:T(128)}, f32[8,5,3,128]{3,2,1,0:T(4,128)S(1)}, f32[8,5,3,128]{3,2,1,0:T(4,128)S(1)}, f32[8,5,3,128,64]{3,4,2,1,0:T(8,128)}, s32[]{:T(128)}, ...) while((s32[]{:T(128)}, f32[8,5,3,128]{3,2,1,0:T(4,128)S(1)}, ...), condition=%wide.region_4.5_spmd.clone, body=%wide.region_1.4_spmd.clone.sunk | while | flops 1059780992 | bytes 97455352 | solution.py:150
  248.4 10.0 fusion.164
  281.0 81.4 %all-gather.24.cloned.1.call-done = bf16[960,2560]{1,0:T(8,128)(2,1)} async-done(((bf16[960,640]{1,0:T(8,128)(2,1)}), bf16[960,2560]{1,0:T(8,128)(2,1)}) %all-gather.24.cloned.1.call-update) | async-done | bytes 4915216 | tf_op jit(solution)/shard_map/all_gather | solution.py:163
  362.4 11.3 fusion.59
  373.7 81.4 %all-gather.20.cloned.1.call-done = bf16[960,2560]{1,0:T(8,128)(2,1)} async-done(((bf16[960,640]{1,0:T(8,128)(2,1)}), bf16[960,2560]{1,0:T(8,128)(2,1)}) %all-gather.20.cloned.1.call-update) | async-done | bytes 4915216 | tf_op jit(solution)/shard_map/all_gather | solution.py:162
  455.0 10.9 fusion.61
  465.9 81.8 %all-gather.28.cloned.1.call-done = bf16[2560,960]{0,1:T(8,128)(2,1)} async-done(((bf16[640,960]{0,1:T(8,128)(2,1)}), bf16[2560,960]{0,1:T(8,128)(2,1)}) %all-gather.28.cloned.1.call-update) | async-done | bytes 4915216 | tf_op jit(solution)/shard_map/all_gather | solution.py:164
  547.7 19.7 multiply_convert_fusion
  605.7 13.8 broadcast_in_dim.34
  619.5 42.2 %while.29 = (s32[]{:T(128)}, f32[8,5,3,128,64]{3,4,2,1,0:T(8,128)}, f32[8,2048,640]{1,2,0:T(8,128)}, s32[]{:T(128)}, bf16[8,2048,640]{1,2,0:T(8,128)(2,1)}, /*in...) while((s32[]{:T(128)}, f32[8,5,3,128,64]{3,4,2,1,0:T(8,128)}, ...), condition=%wide.region_9.10_spmd.clone, body=%wide.region_8.9_spmd.clone.sunk | while | flops 2560197120 | bytes 148397328 | solution.py:253
  629.3 10.4 fusion.177
  663.2 10.1 fusion.51
  674.8 10.1 fusion.55
  685.0 10.2 fusion.57
  715.2 638.5 %reduce-scatter.20.cloned.1.call-done = f32[8,128,640]{1,2,0:T(8,128)} async-done(((f32[8,2048,640]{1,2,0:T(8,128)}), f32[8,128,640]{1,2,0:T(8,128)}) %reduce-scatter.20.cloned.1.call-update) | async-done | bytes 2621456 | tf_op jit(solution)/shard_map/reduce_scatter | solution.py:254
  1373.2 149.6 %reduce-scatter.28.cloned.1.call-done = f32[640,960]{0,1:T(8,128)} async-done(((f32[2560,960]{0,1:T(8,128)}), f32[640,960]{0,1:T(8,128)}) %reduce-scatter.28.cloned.1.call-update) | async-done | bytes 2457616 | tf_op jit(solution)/shard_map/reduce_scatter | solution.py:189
  1522.9 170.8 %reduce-scatter.26.cloned.1.call-done = f32[960,640]{1,0:T(8,128)} async-done(((f32[960,2560]{1,0:T(8,128)}), f32[960,640]{1,0:T(8,128)}) %reduce-scatter.26.cloned.1.call-update) | async-done | bytes 2457616 | tf_op jit(solution)/shard_map/reduce_scatter | solution.py:188
  1693.7 170.8 %reduce-scatter.24.cloned.1.call-done = f32[960,640]{1,0:T(8,128)} async-done(((f32[960,2560]{1,0:T(8,128)}), f32[960,640]{1,0:T(8,128)}) %reduce-scatter.24.cloned.1.call-update) | async-done | bytes 2457616 | tf_op jit(solution)/shard_map/reduce_scatter | solution.py:187
  1865.2 54.1 %reduce-scatter.30.cloned.1.call-done = f32[120,960]{1,0:T(8,128)} async-done(((f32[960,960]{1,0:T(8,128)}), f32[120,960]{1,0:T(8,128)}) %reduce-scatter.30.cloned.1.call-update) | async-done | bytes 460816
  1921.3 65.9 %all-reduce.17.cloned.1.call-done = (f32[960,320]{0,1:T(8,128)}, f32[960,320]{0,1:T(8,128)}) async-done(((f32[960,320]{0,1:T(8,128)}, f32[960,320]{0,1:T(8,128)}), (f32[960,320]{0,1:T(8,128)}, f32[960,320]{0,1:T(8,128)})) %all-reduce.17.cloned.1.call-update) | async-done | bytes 2457616
  1990.7 50.2 %reduce-scatter.22.cloned.1.call-done = f32[120,960]{1,0:T(8,128)} async-done(((f32[960,960]{1,0:T(8,128)}), f32[120,960]{1,0:T(8,128)}) %reduce-scatter.22.cloned.1.call-update) | async-done | bytes 460816 | tf_op jit(solution)/shard_map/reduce_scatter | solution.py:279
  2040.9 13.0 all-reduce.9
  2054.0 12.2 all-reduce.11
  2072.4 15.6 reduce-scatter.36.cloned.1.call-done
  2087.9 47.1 %reduce-scatter.34.cloned.1.call-done = f32[120,640]{1,0:T(8,128)} async-done(((f32[960,640]{1,0:T(8,128)}), f32[120,640]{1,0:T(8,128)}) %reduce-scatter.34.cloned.1.call-update) | async-done | bytes 307216
  2135.0 47.3 %reduce-scatter.32.cloned.1.call-done = f32[120,640]{1,0:T(8,128)} async-done(((f32[960,640]{1,0:T(8,128)}), f32[120,640]{1,0:T(8,128)}) %reduce-scatter.32.cloned.1.call-update) | async-done | bytes 307216
  2182.3 64.4 %all-reduce.19.cloned.1.call-done = (f32[120,960]{1,0:T(8,128)}, f32[120,320]{0,1:T(8,128)}, f32[120,320]{0,1:T(8,128)}, f32[960,120]{1,0:T(8,128)}) async-done(((f32[120,960]{1,0:T(8,128)}, f32[120,320]{0,1:T(8,128)}, f32[120,320]{0,1:T(8,128)}, f32[960,120]{1,0:T(8,128)}), (f32[120,960]{1,0:T(8,128)}, f32[120,320]{0,1:T(8,128)}, f32[120,320]{0,1:T(8,128)}, ...) | async-done | bytes 1228816 | tf_op jit(solution)/shard_map/psum | solution.py:288
  (220 shorter events, 204.3 us)
Async XLA Ops:
  7.2 33.1 %copy-start.28 = (bf16[120,320]{0,1:T(8,128)(2,1)S(1)}, bf16[120,320]{0,1:T(8,128)(2,1)}, u32[]{:S(2)}) copy-start(bf16[120,320]{0,1:T(8,128)(2,1)} %param.19) | copy-start | bytes 230404
  7.2 44.6 %copy-start.8 = (bf16[8,128,960]{1,2,0:T(8,128)(2,1)S(1)}, bf16[8,128,960]{1,2,0:T(8,128)(2,1)}, u32[]{:S(2)}) copy-start(bf16[8,128,960]{1,2,0:T(8,128)(2,1)} %param.15) | copy-start | bytes 5898244
  7.2 50.2 %all-gather.22.cloned.1.call-start = ((), (), s32[]{:S(2)}) async-start(), calls=%async_computation.14 | async-start | bytes 1382400 | tf_op jit(solution)/shard_map/all_gather | solution.py:63
  7.9 56.3 %all-gather.18.cloned.1.call-start = ((), (), s32[]{:S(2)}) async-start(), calls=%async_computation.12 | async-start | bytes 1382400 | tf_op jit(solution)/shard_map/all_gather | solution.py:62
  8.7 81.7 %all-gather.26.cloned.1.call-start = ((), (), s32[]{:S(2)}) async-start(), calls=%async_computation.16 | async-start | bytes 1382400 | tf_op jit(solution)/shard_map/all_gather | solution.py:64
  9.4 110.1 %all-gather.14.cloned.1.call-start = ((), (), s32[]{:S(2)}) async-start(), calls=%async_computation.10 | async-start | bytes 2211840 | tf_op jit(solution)/shard_map/all_gather | solution.py:57
  10.0 226.8 %all-gather.12.cloned.1.call-start = ((), (), s32[]{:S(2)}) async-start(), calls=%async_computation.9 | async-start | bytes 22282240 | tf_op jit(solution)/shard_map/all_gather | solution.py:121
  29.0 94.4 %copy-start.30 = (f32[960]{0:T(1024)}, f32[960]{0:T(1024)S(1)}, u32[]{:S(2)}) copy-start(f32[960]{0:T(1024)S(1)} %convert_element_type.107) | copy-start | bytes 11524
  40.3 13.7 copy-start.13
  52.2 71.1 %copy-start.32 = (f32[8,128]{1,0:T(8,128)}, f32[8,128]{1,0:T(8,128)S(1)}, u32[]{:S(2)}) copy-start(f32[8,128]{1,0:T(8,128)S(1)} %add_rsqrt_fusion.1) | copy-start | bytes 12292
  53.0 74.3 %copy-start.24 = (f32[128,32]{0,1:T(8,128)}, f32[128,32]{0,1:T(8,128)S(1)}, u32[]{:S(2)}) copy-start(f32[128,32]{0,1:T(8,128)S(1)} %get-tuple-element.266) | copy-start | bytes 49156
  56.4 215.9 %all-gather.16.cloned.1.call-start = ((), (), s32[]{:S(2)}) async-start(), calls=%async_computation.11 | async-start | bytes 2211840 | tf_op jit(solution)/shard_map/all_gather | solution.py:60
  57.3 305.1 %all-gather.24.cloned.1.call-start = ((), (), s32[]{:S(2)}) async-start(), calls=%async_computation.15 | async-start | bytes 6144000 | tf_op jit(solution)/shard_map/all_gather | solution.py:163
  58.0 397.0 %all-gather.20.cloned.1.call-start = ((), (), s32[]{:S(2)}) async-start(), calls=%async_computation.13 | async-start | bytes 6144000 | tf_op jit(solution)/shard_map/all_gather | solution.py:162
  64.2 483.5 %all-gather.28.cloned.1.call-start = ((), (), s32[]{:S(2)}) async-start(), calls=%async_computation.17 | async-start | bytes 6144000 | tf_op jit(solution)/shard_map/all_gather | solution.py:164
  90.4 1263.3 %reduce-scatter.20.cloned.1.call-start = ((), (), s32[]{:S(2)}) async-start(), calls=%async_computation.18 | async-start | bytes 44564480 | tf_op jit(solution)/shard_map/reduce_scatter | solution.py:254
  248.4 10.1 copy-start.4
  567.5 18.2 slice-start
  567.5 18.2 slice-start.2
  605.7 13.8 copy-start.29
  661.7 861.1 %reduce-scatter.28.cloned.1.call-start = ((), (), s32[]{:S(2)}) async-start(), calls=%async_computation.22 | async-start | bytes 12288000 | tf_op jit(solution)/shard_map/reduce_scatter | solution.py:189
  673.3 1020.3 %reduce-scatter.26.cloned.1.call-start = ((), (), s32[]{:S(2)}) async-start(), calls=%async_computation.21 | async-start | bytes 12288000 | tf_op jit(solution)/shard_map/reduce_scatter | solution.py:188
  684.9 1179.5 %reduce-scatter.24.cloned.1.call-start = ((), (), s32[]{:S(2)}) async-start(), calls=%async_computation.20 | async-start | bytes 12288000 | tf_op jit(solution)/shard_map/reduce_scatter | solution.py:187
  695.2 1224.1 %reduce-scatter.30.cloned.1.call-start = ((), (), s32[]{:S(2)}) async-start(), calls=%async_computation.23 | async-start | bytes 4423680
  703.0 1284.2 %all-reduce.17.cloned.1.call-start = ((), (), s32[]{:S(2)}) async-start(), calls=%async_computation.27 | async-start | bytes 5242880
  715.2 640.7 %copy-start.14 = (bf16[960,320]{0,1:T(8,128)(2,1)S(1)}, bf16[960,320]{0,1:T(8,128)(2,1)}, u32[]{:S(2)}) copy-start(bf16[960,320]{0,1:T(8,128)(2,1)} %copy-done.13) | copy-start | bytes 1843204
  1366.5 674.3 %reduce-scatter.22.cloned.1.call-start = ((), (), s32[]{:S(2)}) async-start(), calls=%async_computation.19 | async-start | bytes 4423680 | tf_op jit(solution)/shard_map/reduce_scatter | solution.py:279
  1373.1 714.8 %reduce-scatter.36.cloned.1.call-start = ((), (), s32[]{:S(2)}) async-start(), calls=%async_computation.26 | async-start | bytes 2764800
  1522.8 612.2 %reduce-scatter.34.cloned.1.call-start = ((), (), s32[]{:S(2)}) async-start(), calls=%async_computation.25 | async-start | bytes 2764800
  1693.6 347.3 %copy-start.34 = (f32[960]{0:T(1024)S(1)}, f32[960]{0:T(1024)}, u32[]{:S(2)}) copy-start(f32[960]{0:T(1024)} %get-tuple-element.189) | copy-start | bytes 11524
  1693.7 488.6 %reduce-scatter.32.cloned.1.call-start = ((), (), s32[]{:S(2)}) async-start(), calls=%async_computation.24 | async-start | bytes 2764800
  1864.5 382.1 %all-reduce.19.cloned.1.call-start = ((), (), s32[]{:S(2)}) async-start(), calls=%async_computation.28 | async-start | bytes 2621440 | tf_op jit(solution)/shard_map/psum | solution.py:288
  (29 other events, 96.4 us)
Sparse Core Ops, SparseCore 0:
  9.9 28.1 all-gather.21
  40.0 24.1 all-gather.17
  66.1 24.2 all-gather.25
  92.1 27.3 all-gather.13
  121.4 115.3 all-gather.11
  239.1 28.9 all-gather.15
  269.7 92.6 all-gather.23
  363.9 91.0 all-gather.19
  456.6 91.0 all-gather.27
  661.8 691.8 reduce-scatter.19
  1356.1 166.6 reduce-scatter.27
  1525.1 168.4 reduce-scatter.25
  1696.0 168.4 reduce-scatter.23
  1868.3 50.9 reduce-scatter.29
  1922.4 64.7 all-reduce.16
  1991.1 49.6 reduce-scatter.21
  2045.1 42.7 reduce-scatter.35
  2092.2 42.8 reduce-scatter.33
  2139.4 42.8 reduce-scatter.31
  2185.5 61.0 all-reduce.18
where the time goes:
time: 2270 us; the launch traced here: 2260 us
  waiting for transfers between devices  1890 us (83%)
  matrix products  175 us (8%)
  local copies, waits for them, and re-layouts  68.3 us (3%)
  blocking collectives  60.4 us (3%)
  other arithmetic  46.5 us (2%)
    reduce_scatter x1, waiting for transfers between devices, body(): lax.psum_scatter(dkv_all, ('context', 'tensor'), scatter_dimension=1, til...  639 us
    unnamed x25, waiting for transfers between devices  233 us
    reduce_scatter x1, waiting for transfers between devices, body(): lax.psum_scatter(grad_gate_part, 'tensor', scatter_dimension=1, tiled=True)  171 us
    reduce_scatter x1, waiting for transfers between devices, body(): lax.psum_scatter(grad_up_part, 'tensor', scatter_dimension=1, tiled=True)  171 us
    reduce_scatter x1, waiting for transfers between devices, body(): lax.psum_scatter(grad_down_part, 'tensor', scatter_dimension=0, tiled=True)  150 us
    all_gather x1, waiting for transfers between devices, body(): lax.all_gather(key_value, ('context', 'tensor'), axis=1, tiled=True)  109 us
    all_gather x1, waiting for transfers between devices, body(): lax.all_gather(w_down_all, 'tensor', axis=0, tiled=True)  81.8 us
    all_gather x1, waiting for transfers between devices, body(): lax.all_gather(w_up_all, 'tensor', axis=1, tiled=True)  81.4 us
  transfers between devices with their start and end apart: 20, of which 18 were waited for; matrix products, arithmetic and copies ran while one was open for 7% of the time, Pallas kernels for 0%

commit v1 on v0

v1 whole, which is shorter than its diff:
```python
import math

import jax
import jax.numpy as jnp
from jax import lax
from jax.experimental import pallas as pl
from jax.experimental.pallas import tpu as pltpu
from jax.sharding import PartitionSpec as P

HEADS = 15
KV_HEADS = 5
HEAD_DIM = 64


epsilon = 1e-05
rope_base = 10000.0
neg_large = -1e30


def rms_scale(values):
    return lax.rsqrt(jnp.mean(values * values, axis=-1, keepdims=True) + epsilon)


def tables(positions):
    step_index = jnp.arange(HEAD_DIM // 2).astype(jnp.float32)
    frequency = jnp.power(rope_base, -2.0 * step_index / HEAD_DIM)
    angles = positions.astype(jnp.float32)[:, None] * frequency[None, :]
    return (jnp.cos(angles), jnp.sin(angles))


def rotate(values, cos_t, sin_t):
    half_dim = values.shape[-1] // 2
    first_half = values[..., :half_dim]
    second_half = values[..., half_dim:]
    return jnp.concatenate(
        [first_half * cos_t - second_half * sin_t, second_half * cos_t + first_half * sin_t],
        axis=-1,
    )


def contract_rows(left_mat, right_mat):
    return lax.dot_general(
        left_mat, right_mat, (((0,), (0,)), ((), ())), preferred_element_type=jnp.float32
    )


def contract_cols(left_mat, right_mat):
    return lax.dot_general(
        left_mat, right_mat, (((1,), (1,)), ((), ())), preferred_element_type=jnp.float32
    )


def bits_of(axis_name):
    return [1 << k for k in range(int(math.log2(lax.axis_size(axis_name))))]


def swap(values, axis_name, bit):
    size = lax.axis_size(axis_name)
    return lax.ppermute(values, axis_name, [(i, i ^ bit) for i in range(size)])


def reduce_rows(partial, order):
    fsdp, context = (lax.axis_size("fsdp"), lax.axis_size("context"))
    names = [("fsdp", b) for b in reversed(bits_of("fsdp"))]
    names += [("context", b) for b in reversed(bits_of("context"))]
    rows, columns = partial.shape
    block = partial.astype(jnp.bfloat16).reshape(
        (2,) * len(names) + (rows // (fsdp * context), columns)
    )
    for step in order:
        dim = names.index(step)
        names.pop(dim)
        axis_name, bit = step
        mine = (lax.axis_index(axis_name) // bit) % 2
        sent = lax.dynamic_index_in_dim(block, 1 - mine, dim, keepdims=False)
        kept = lax.dynamic_index_in_dim(block, mine, dim, keepdims=False)
        arrived = swap(sent, axis_name, bit)
        block = (kept.astype(jnp.float32) + arrived.astype(jnp.float32)).astype(jnp.bfloat16)
    return block


def orders():
    core = [("context", b) for b in bits_of("context")[:1]]
    chips = [("context", b) for b in bits_of("context")[1:]]
    outer = [("fsdp", b) for b in bits_of("fsdp")]
    return (core + chips + outer, core + outer + chips)


def reduce_units(block):
    rows, columns = block.shape
    size = lax.axis_size("tensor")
    parts = jnp.transpose(block.reshape(rows, size, columns // size), (1, 0, 2))
    for bit in bits_of("tensor"):
        mine = (lax.axis_index("tensor") // bit) % 2
        pairs = parts.reshape((parts.shape[0] // 2, 2) + parts.shape[1:])
        sent = lax.dynamic_index_in_dim(pairs, 1 - mine, 1, keepdims=False)
        kept = lax.dynamic_index_in_dim(pairs, mine, 1, keepdims=False)
        arrived = swap(sent, "tensor", bit)
        total = kept.astype(jnp.float32) + arrived.astype(jnp.float32)
        parts = total.astype(jnp.bfloat16)
    return total.reshape(rows, columns // size)


def reduce_copies(block):
    for bit in bits_of("tensor"):
        arrived = swap(block, "tensor", bit)
        total = block.astype(jnp.float32) + arrived.astype(jnp.float32)
        block = total.astype(jnp.bfloat16)
    return total


def to_sequences(rows):
    context = lax.axis_size("context")
    seqs, count, width = rows.shape
    parts = rows.reshape(context, seqs // context, count, width)
    moved = lax.all_to_all(parts, "context", 0, 0, tiled=False)
    return jnp.transpose(moved, (1, 0, 2, 3))


def to_positions(rows):
    context = lax.axis_size("context")
    seqs, blocks, count, width = rows.shape
    parts = jnp.transpose(rows, (1, 0, 2, 3))
    moved = lax.all_to_all(parts, "context", 0, 0, tiled=False)
    return moved.reshape(context * seqs, count, width)


def dot32(left_mat, right_mat):
    return jnp.dot(left_mat, right_mat, preferred_element_type=jnp.float32)


def attend_kernel(span, q_t_ref, key_ref, v_t_ref, bias_ref, out_ref, log_ref):
    chunk = pl.program_id(1)
    q_t = q_t_ref[0, 0]
    columns = q_t.shape[1]

    def one_block(block_index, state, bias):
        top_run, sum_run, acc_run = state
        rows = pl.ds(pl.multiple_of(block_index * span, span), span)
        scores = dot32(key_ref[0, rows, :], q_t)
        if bias is not None:
            scores = scores + bias
        top_new = jnp.maximum(top_run, jnp.max(scores, axis=0, keepdims=True))
        expo = jnp.exp(scores - top_new)
        shrink = jnp.exp(top_run - top_new)
        sum_new = sum_run * shrink + jnp.sum(expo, axis=0, keepdims=True)
        mixed = dot32(v_t_ref[0, block_index], expo.astype(jnp.bfloat16))
        return (top_new, sum_new, acc_run * shrink + mixed)

    state = (
        jnp.full((1, columns), neg_large, jnp.float32),
        jnp.zeros((1, columns), jnp.float32),
        jnp.zeros((HEAD_DIM, columns), jnp.float32),
    )
    state = one_block(chunk, state, bias_ref[...])
    top, total, acc = lax.fori_loop(0, chunk, lambda j, s: one_block(j, s, None), state)
    out_ref[0, 0] = acc / total
    log_ref[0, 0] = top + jnp.log(total)


def back_kernel(
    span,
    q_ref,
    q_t_ref,
    do_ref,
    do_t_ref,
    out_ref,
    log_ref,
    key_ref,
    k_t_ref,
    value_ref,
    bias_ref,
    dq_ref,
    dk_ref,
    dv_ref,
):
    chunk = pl.program_id(1)

    @pl.when(chunk == 0)
    def _():
        dk_ref[...] = jnp.zeros_like(dk_ref)
        dv_ref[...] = jnp.zeros_like(dv_ref)

    queries = q_ref[0, 0]
    q_t = q_t_ref[0, 0]
    d_out = do_ref[0, 0]
    d_out_t = do_t_ref[0, 0]
    log_sum = log_ref[0, 0]
    delta = jnp.sum(d_out_t.astype(jnp.float32) * out_ref[0, 0], axis=0, keepdims=True)

    def one_block(block_index, dq_acc, bias):
        rows = pl.ds(pl.multiple_of(block_index * span, span), span)
        scores = dot32(key_ref[0, rows, :], q_t)
        if bias is not None:
            scores = scores + bias
        probs = jnp.exp(scores - log_sum)
        d_probs = dot32(value_ref[0, rows, :], d_out_t)
        d_scores = (probs * (d_probs - delta)).astype(jnp.bfloat16)
        dv_ref[0, rows, :] += dot32(probs.astype(jnp.bfloat16), d_out)
        dk_ref[0, rows, :] += dot32(d_scores, queries)
        return dq_acc + dot32(k_t_ref[0, block_index], d_scores)

    dq_acc = one_block(chunk, jnp.zeros(q_t.shape, jnp.float32), bias_ref[...])
    dq_acc = lax.fori_loop(0, chunk, lambda j, s: one_block(j, s, None), dq_acc)
    dq_ref[0, 0] = dq_acc * (1.0 / math.sqrt(HEAD_DIM))


def per_chunk(*shape):
    return pl.BlockSpec((1, 1) + shape, lambda h, c: (h, c, 0, 0))


def per_head(*shape):
    return pl.BlockSpec((1,) + shape, lambda h, c: (h,) + (0,) * len(shape))


def whole(*shape):
    return pl.BlockSpec(shape, lambda h, c: (0,) * len(shape))


def attend(q_t, keys, v_t, bias):
    heads, chunks, dim, columns = q_t.shape
    span = bias.shape[0]
    length = keys.shape[1]
    pairs = heads * columns * span * chunks * (chunks + 1) // 2
    return pl.pallas_call(
        lambda *refs: attend_kernel(span, *refs),
        grid=(heads, chunks),
        in_specs=[
            per_chunk(dim, columns),
            per_head(length, dim),
            per_head(chunks, dim, span),
            whole(span, columns),
        ],
        out_specs=[per_chunk(dim, columns), per_chunk(1, columns)],
        out_shape=[
            jax.ShapeDtypeStruct((heads, chunks, dim, columns), jnp.float32),
            jax.ShapeDtypeStruct((heads, chunks, 1, columns), jnp.float32),
        ],
        cost_estimate=pl.CostEstimate(
            flops=16 * dim * pairs, bytes_accessed=8 * q_t.size, transcendentals=pairs
        ),
        compiler_params=pltpu.CompilerParams(vmem_limit_bytes=40 * 1024 * 1024),
        name="attend",
    )(q_t, keys, v_t, bias)


def attend_back(queries, q_t, d_out, d_out_t, out, log_sum, keys, k_t, values, bias):
    heads, chunks, dim, columns = q_t.shape
    span = bias.shape[0]
    length = keys.shape[1]
    pairs = heads * columns * span * chunks * (chunks + 1) // 2
    return pl.pallas_call(
        lambda *refs: back_kernel(span, *refs),
        grid=(heads, chunks),
        in_specs=[
            per_chunk(columns, dim),
            per_chunk(dim, columns),
            per_chunk(columns, dim),
            per_chunk(dim, columns),
            per_chunk(dim, columns),
            per_chunk(1, columns),
            per_head(length, dim),
            per_head(chunks, dim, span),
            per_head(length, dim),
            whole(span, columns),
        ],
        out_specs=[per_chunk(dim, columns), per_head(length, dim), per_head(length, dim)],
        out_shape=[
            jax.ShapeDtypeStruct((heads, chunks, dim, columns), jnp.float32),
            jax.ShapeDtypeStruct((heads, length, dim), jnp.float32),
            jax.ShapeDtypeStruct((heads, length, dim), jnp.float32),
        ],
        cost_estimate=pl.CostEstimate(
            flops=40 * dim * pairs, bytes_accessed=16 * q_t.size, transcendentals=pairs
        ),
        compiler_params=pltpu.CompilerParams(vmem_limit_bytes=40 * 1024 * 1024),
        name="attend_back",
    )(queries, q_t, d_out, d_out_t, out, log_sum, keys, k_t, values, bias)


def body(
    tokens, gain_attn, w_query, w_key, w_value, w_out, gain_mlp, w_gate, w_up, w_down, cotangent
):
    seq_count, row_count, model_width = tokens.shape
    group_size = HEADS // KV_HEADS
    kv_width = KV_HEADS * HEAD_DIM
    q_width = HEADS * HEAD_DIM
    inv_root = 1.0 / math.sqrt(HEAD_DIM)
    rows_axes = ("fsdp", "context")
    chunks = lax.axis_size("context")
    turns = lax.axis_size("tensor")
    seqs = seq_count // chunks
    own_rows = w_query.shape[0]
    gains = jnp.stack([gain_attn, gain_mlp] + [jnp.zeros_like(gain_attn)] * 126, axis=1)
    attn_pack = jnp.concatenate([w_query, w_key, w_value, w_out.T, gains], axis=1)
    attn_all = lax.all_gather(attn_pack, rows_axes, axis=0, tiled=True)
    in_seq = to_sequences(tokens)
    mlp_pack = jnp.stack([w_gate, w_up, w_down.T])
    mlp_all = lax.all_gather(mlp_pack, ("fsdp", "context", "tensor"), axis=0, tiled=False)
    cot_seq = to_sequences(cotangent)
    w_qkv = attn_all[:, : q_width + 2 * kv_width]
    w_out_t = attn_all[:, q_width + 2 * kv_width : 2 * q_width + 2 * kv_width]
    gain_columns = attn_all[:, 2 * q_width + 2 * kv_width :].astype(jnp.float32)
    g_attn = gain_columns[:, 0]
    g_mlp = gain_columns[:, 1]

    block_start = lax.axis_index("tensor") * row_count
    span = turns * row_count
    positions = (
        jnp.arange(chunks)[:, None] * span + block_start + jnp.arange(row_count)[None, :]
    ).reshape(-1)
    cos_t, sin_t = tables(positions)
    cos_b = cos_t[:, None, :]
    sin_b = sin_t[:, None, :]
    local_rows = chunks * row_count
    query_place = jnp.tile(block_start + jnp.arange(row_count), group_size)
    bias = jnp.where(jnp.arange(span)[:, None] <= query_place[None, :], 0.0, neg_large)
    bias = bias.astype(jnp.float32)

    inputs = in_seq.reshape(seqs, local_rows, model_width).astype(jnp.float32)
    rms_attn = rms_scale(inputs)
    flat_attn = (inputs * rms_attn * g_attn).astype(jnp.bfloat16).reshape(-1, model_width)
    qkv = dot32(flat_attn, w_qkv).reshape(seqs, local_rows, HEADS + 2 * KV_HEADS, HEAD_DIM)
    turned = rotate(qkv[:, :, : HEADS + KV_HEADS], cos_b, sin_b)
    queries = (turned[:, :, :HEADS] * inv_root).astype(jnp.bfloat16)
    key_value = jnp.concatenate(
        [turned[:, :, HEADS:].astype(jnp.bfloat16), qkv[:, :, HEADS + KV_HEADS :].astype(jnp.bfloat16)],
        axis=2,
    ).reshape(seqs, chunks, row_count, 2 * kv_width)

    def rows_major(part):
        parts = part.reshape(chunks, row_count, KV_HEADS, group_size, HEAD_DIM)
        return jnp.transpose(parts, (2, 0, 3, 1, 4)).reshape(
            KV_HEADS, chunks, group_size * row_count, HEAD_DIM
        )

    def columns_major(part):
        parts = part.reshape(chunks, row_count, KV_HEADS, group_size, HEAD_DIM)
        return jnp.transpose(parts, (2, 0, 4, 3, 1)).reshape(
            KV_HEADS, chunks, HEAD_DIM, group_size * row_count
        )

    def from_columns(part):
        parts = part.reshape(KV_HEADS, chunks, HEAD_DIM, group_size, row_count)
        return jnp.transpose(parts, (1, 4, 0, 3, 2)).reshape(local_rows, HEADS, HEAD_DIM)

    saved = []
    heads_list = []
    for seq in range(seqs):
        gathered = lax.all_gather(key_value[seq], "tensor", axis=0, tiled=False)
        kv = gathered.reshape(turns, chunks, row_count, 2, KV_HEADS, HEAD_DIM)
        kv_rows = jnp.transpose(kv, (3, 4, 1, 0, 2, 5)).reshape(
            2, KV_HEADS, chunks * span, HEAD_DIM
        )
        kv_cols = jnp.transpose(kv, (3, 4, 1, 5, 0, 2)).reshape(
            2, KV_HEADS, chunks, HEAD_DIM, span
        )
        q_t = columns_major(queries[seq])
        out, log_sum = attend(q_t, kv_rows[0], kv_cols[1], bias)
        saved.append((q_t, out, log_sum, kv_rows, kv_cols))
        heads_list.append(from_columns(out.astype(jnp.bfloat16)))
    flat_heads = jnp.stack(heads_list).reshape(-1, q_width)

    branch = contract_cols(flat_heads, w_out_t).reshape(seqs, local_rows, model_width)
    middle = inputs + branch
    rms_mlp = rms_scale(middle)
    flat_mlp = (middle * rms_mlp * g_mlp).astype(jnp.bfloat16).reshape(-1, model_width)
    units = w_gate.shape[1]
    mlp_use = jnp.transpose(
        mlp_all.reshape(model_width // own_rows, turns, 3, own_rows, units), (2, 0, 3, 1, 4)
    ).reshape(3, model_width, turns * units)
    w_gate_use, w_up_use, w_down_t = (mlp_use[0], mlp_use[1], mlp_use[2])
    gate_pre = dot32(flat_mlp, w_gate_use)
    up_pre = dot32(flat_mlp, w_up_use)
    sigma_gate = jax.nn.sigmoid(gate_pre)
    silu_gate = gate_pre * sigma_gate
    hidden = (silu_gate * up_pre).astype(jnp.bfloat16)
    result = middle + contract_cols(hidden, w_down_t).reshape(seqs, local_rows, model_width)
    result_out = to_positions(
        result.astype(jnp.bfloat16).reshape(seqs, chunks, row_count, model_width)
    ).astype(jnp.float32)

    flat_grad = cot_seq.reshape(-1, model_width)
    d_hidden = dot32(flat_grad, w_down_t)
    d_gate = (d_hidden * up_pre * sigma_gate * (1.0 + gate_pre * (1.0 - sigma_gate))).astype(
        jnp.bfloat16
    )
    d_up = (d_hidden * silu_gate).astype(jnp.bfloat16)
    first_order, second_order = orders()
    d_normed = contract_cols(d_gate, w_gate_use) + contract_cols(d_up, w_up_use)
    d_normed = d_normed.reshape(seqs, local_rows, model_width)
    grad_down = reduce_units(reduce_rows(contract_rows(flat_grad, hidden), first_order)).T
    grad_gate = reduce_units(reduce_rows(contract_rows(flat_mlp, d_gate), second_order))
    grad_up = reduce_units(reduce_rows(contract_rows(flat_mlp, d_up), first_order))

    norm_mid = middle * rms_mlp
    scaled_mid = d_normed * g_mlp
    gain_mlp_part = jnp.sum(d_normed * norm_mid, axis=(0, 1))
    d_middle = cot_seq.reshape(seqs, local_rows, model_width).astype(jnp.float32) + rms_mlp * (
        scaled_mid - norm_mid * jnp.mean(scaled_mid * norm_mid, axis=-1, keepdims=True)
    )
    d_branch = d_middle.astype(jnp.bfloat16).reshape(-1, model_width)
    grad_out = reduce_copies(reduce_rows(contract_rows(d_branch, flat_heads), second_order)).T
    d_heads = dot32(d_branch, w_out_t).astype(jnp.bfloat16).reshape(seqs, local_rows, q_width)

    dq_list, dkv_list = ([], [])
    for seq in range(seqs):
        q_t, out, log_sum, kv_rows, kv_cols = saved[seq]
        dq, dk, dv = attend_back(
            rows_major(queries[seq]),
            q_t,
            rows_major(d_heads[seq]),
            columns_major(d_heads[seq]),
            out,
            log_sum,
            kv_rows[0],
            kv_cols[0],
            kv_rows[1],
            bias,
        )
        dq_list.append(from_columns(dq))
        dkv = jnp.stack([dk, dv]).astype(jnp.bfloat16)
        dkv = dkv.reshape(2 * KV_HEADS, chunks, turns, row_count, HEAD_DIM)
        dkv = jnp.transpose(dkv, (2, 1, 3, 0, 4)).reshape(turns, local_rows, 2 * kv_width)
        own = lax.psum_scatter(dkv, "tensor", scatter_dimension=0, tiled=False)
        dkv_list.append(own.reshape(local_rows, 2 * KV_HEADS, HEAD_DIM))
    d_query = jnp.stack(dq_list)
    d_kv = jnp.stack(dkv_list).astype(jnp.float32)
    d_query_lin = rotate(d_query, cos_b, -sin_b).astype(jnp.bfloat16)
    d_key_lin = rotate(d_kv[:, :, :KV_HEADS], cos_b, -sin_b).astype(jnp.bfloat16)
    d_value_lin = d_kv[:, :, KV_HEADS:].astype(jnp.bfloat16)
    d_q_flat = d_query_lin.reshape(-1, q_width)
    d_kv_flat = jnp.concatenate([d_key_lin, d_value_lin], axis=2).reshape(-1, 2 * kv_width)
    d_normed_attn = contract_cols(d_q_flat, w_qkv[:, :q_width]) + contract_cols(
        d_kv_flat, w_qkv[:, q_width:]
    )
    d_normed_attn = d_normed_attn.reshape(seqs, local_rows, model_width)
    grad_query = reduce_copies(reduce_rows(contract_rows(flat_attn, d_q_flat), first_order))
    grad_kv = reduce_copies(reduce_rows(contract_rows(flat_attn, d_kv_flat), second_order))
    norm_in = inputs * rms_attn
    scaled_in = d_normed_attn * g_attn
    gain_attn_part = jnp.sum(d_normed_attn * norm_in, axis=(0, 1))
    grad_tokens = d_middle + rms_attn * (
        scaled_in - norm_in * jnp.mean(scaled_in * norm_in, axis=-1, keepdims=True)
    )
    grad_tokens_out = to_positions(
        grad_tokens.astype(jnp.bfloat16).reshape(seqs, chunks, row_count, model_width)
    ).astype(jnp.float32)
    gain_sums = lax.psum(
        jnp.stack([gain_attn_part, gain_mlp_part]), ("fsdp", "context", "tensor")
    )
    own_gains = lax.dynamic_slice_in_dim(
        gain_sums, lax.axis_index(rows_axes) * own_rows, own_rows, 1
    )
    return (
        result_out,
        grad_tokens_out,
        own_gains[0],
        grad_query,
        grad_kv[:, :kv_width],
        grad_kv[:, kv_width:],
        grad_out,
        own_gains[1],
        grad_gate,
        grad_up,
        grad_down,
    )


def solution(mesh):
    placed = (
        P("fsdp", ("context", "tensor"), None),
        P(("fsdp", "context")),
        P(("fsdp", "context"), None),
        P(("fsdp", "context"), None),
        P(("fsdp", "context"), None),
        P(None, ("fsdp", "context")),
        P(("fsdp", "context")),
        P(("fsdp", "context"), "tensor"),
        P(("fsdp", "context"), "tensor"),
        P("tensor", ("fsdp", "context")),
        P("fsdp", ("context", "tensor"), None),
    )
    return jax.shard_map(
        body,
        mesh=mesh,
        in_specs=placed,
        out_specs=(
            P("fsdp", ("context", "tensor"), None),
            P("fsdp", ("context", "tensor"), None),
            P(("fsdp", "context")),
            P(("fsdp", "context"), None),
            P(("fsdp", "context"), None),
            P(("fsdp", "context"), None),
            P(None, ("fsdp", "context")),
            P(("fsdp", "context")),
            P(("fsdp", "context"), "tensor"),
            P(("fsdp", "context"), "tensor"),
            P("tensor", ("fsdp", "context")),
        ),
        check_vma=False,
    )
```

time: 2270 us -> 1040 us (0.46)
  waiting for transfers between devices: 1890 us -> 228 us
  local copies, waits for them, and re-layouts: 68.3 us -> 370 us
  Pallas kernels: 0 us -> 129 us
  matrix products: 175 us -> 121 us
  starting transfers between devices: 1.18 us -> 47.2 us
  other arithmetic: 46.5 us -> 77.1 us
    reduce_scatter x5 -> x2, waiting for transfers between devices: 1180 us -> 0.01 us  [body(): own = lax.psum_scatter(dkv, 'tensor', scatter_dimension=0, tiled=False)]
    all_gather x9 -> x4, waiting for transfers between devices: 411 us -> 10.3 us  [the longest x1 10.3 us: body(): attn_all = lax.all_gather(attn_pack, rows_axes, axis=0, tiled=True)]
    unnamed x25 -> x6, waiting for transfers between devices: 233 us -> 0.6 us
    ppermute x0 -> x30, waiting for transfers between devices: none -> 159 us  [swap(): return lax.ppermute(values, axis_name, [(i, i ^ bit) for i in range(size)])]
    pallas_call x0 -> x4, Pallas kernels: none -> 129 us  [the longest x2 72.4 us: attend_back(): pl.pallas_call(lambda *refs: back_kernel(span, *refs), grid=(heads, chunk...]
    reshape x0 -> x20, local copies, waits for them, and re-layouts: none -> 78.2 us  [the longest x1 22.5 us: body(): mlp_all.reshape(model_width // own_rows, turns, 3, own_rows, units)]
    psum x1 -> x0, waiting for transfers between devices: 64.4 us -> none  [body(): lax.psum((shards[0], shards[1], shards[2], shards[3], shards[4], shards[5...]
    all_to_all x0 -> x4, waiting for transfers between devices: none -> 58.1 us  [the longest x2 58.1 us: to_sequences(): moved = lax.all_to_all(parts, 'context', 0, 0, tiled=False)]
  transfers between devices with their start and end apart: 20 -> 40, of which waited for: 18 -> 18; matrix products, arithmetic and copies ran while one was open for 7% -> 32% of each run, Pallas kernels for 0% -> 13%
where the time goes in v1:
time: 1040 us; the launch traced here: 1030 us
  local copies, waits for them, and re-layouts  370 us (36%)
  waiting for transfers between devices  228 us (22%)
  Pallas kernels  129 us (12%)
  matrix products  121 us (12%)
  other arithmetic  77.1 us (7%)
  starting transfers between devices  47.2 us (5%)
  blocking collectives  39.8 us (4%)
  between operations  16 us (2%)
    ppermute x30, waiting for transfers between devices, swap(): return lax.ppermute(values, axis_name, [(i, i ^ bit) for i in range(size)])  159 us
    pallas_call x2, Pallas kernels, attend_back(): pl.pallas_call(lambda *refs: back_kernel(span, *refs), grid=(heads, chunk...  72.4 us
    unnamed x174, local copies, waits for them, and re-layouts  64.1 us
    all_to_all x2, waiting for transfers between devices, to_sequences(): moved = lax.all_to_all(parts, 'context', 0, 0, tiled=False)  58.1 us
    pallas_call x2, Pallas kernels, attend(): pl.pallas_call(lambda *refs: attend_kernel(span, *refs), grid=(heads, chu...  56.4 us
    dot_general x5, matrix products, dot32(): return jnp.dot(left_mat, right_mat, preferred_element_type=jnp.float32)  48.3 us
    dot_general x6, matrix products, contract_cols(): lax.dot_general(left_mat, right_mat, (((1,), (1,)), ((), ())), preferred_...  40 us
    psum x1, blocking collectives, body(): lax.psum(jnp.stack([gain_attn_part, gain_mlp_part]), ('fsdp', 'context',...  39.8 us
  transfers between devices with their start and end apart: 40, of which 18 were waited for; matrix products, arithmetic and copies ran while one was open for 32% of the time, Pallas kernels for 13%

profile of v1, /device:TPU:0, one launch (start us, length us, event | category | flops | bytes accessed | tf_op | source)
XLA Modules:
  0.0 1027.9 jit_solution(5693614208251655888)
XLA Ops:
  23.0 34.7 %all-to-all-done = bf16[4,2,128,960]{2,1,3,0:T(2,128)(2,1)S(1)} async-done(((bf16[4,2,128,960]{2,1,3,0:T(2,128)(2,1)}), bf16[4,2,128,960]{2,1,3,0:T(2,128)(2,1)S(1)}, u32[]{:S(2)}, u32[]{:S(2)}) %all-to-all-start) | async-done | bytes 1966112 | tf_op jit(solution)/shard_map/all_to_all | solution.py:116
  58.1 10.3 all-gather.6.cloned.1.call-done
  115.5 23.5 %all-to-all-done.2 = bf16[4,2,128,960]{2,1,3,0:T(2,128)(2,1)} async-done(((bf16[4,2,128,960]{2,1,3,0:T(2,128)(2,1)}), bf16[4,2,128,960]{2,1,3,0:T(2,128)(2,1)}, u32[]{:S(2)}, u32[]{:S(2)}) %all-to-all-start.2) | async-done | bytes 1966112 | tf_op jit(solution)/shard_map/all_to_all | solution.py:116
  213.5 28.2 %attend.2 = (f32[5,4,64,384]{3,2,1,0:T(8,128)S(1)}, f32[5,4,1,384]{3,2,1,0:T(1,128)S(1)}) custom-call(bf16[5,4,64,384]{3,2,1,0:T(8,128)(2,1)S(1)} %copy-done.17, bf16[5,2048,64]{2,1,0:T(8,128)(2,1)S(1)} %bitcast.435, bf16[5,4,64,512]{3,2,1,0:T(8,128)(2,1)S(1)} %copy-done.15, f32[512,384]{1,0:T(8,128)S(1)} %fusion.49.refs_3_.refs_9_), custom_call_target="tpu_custom_call" | custom-call | flops 10066329600 | bytes 3932160 | tf_op jit(solution)/shard_map/attend/pallas_call | solution.py:225
  281.8 28.2 %attend.3 = (f32[5,4,64,384]{3,2,1,0:T(8,128)S(1)}, f32[5,4,1,384]{3,2,1,0:T(1,128)S(1)}) custom-call(bf16[5,4,64,384]{3,2,1,0:T(8,128)(2,1)S(1)} %copy-done.19, bf16[5,2048,64]{2,1,0:T(8,128)(2,1)S(1)} %bitcast.437, bf16[5,4,64,512]{3,2,1,0:T(8,128)(2,1)S(1)} %copy-done.16, f32[512,384]{1,0:T(8,128)S(1)} %fusion.49.refs_3_.refs_9_), custom_call_target="tpu_custom_call" | custom-call | flops 10066329600 | bytes 3932160 | tf_op jit(solution)/shard_map/attend/pallas_call | solution.py:225
  360.3 22.5 %copy.594 = bf16[8,4,3,120,640]{4,1,3,0,2:T(4,128)(2,1)S(1)} copy(bf16[8,4,3,120,640]{4,3,2,1,0:T(8,128)(2,1)} %bitcast.458) | data formatting | bytes 29491200 | tf_op jit(solution)/shard_map/reshape | solution.py:370
  382.8 7.0 fusion.61
  398.4 8.3 fusion.69
  406.8 8.4 fusion.70
  418.2 20.1 %fusion.3 = (bf16[1024,2560]{1,0:T(8,128)(2,1)}, bf16[1024,2560]{1,0:T(8,128)(2,1)}, bf16[1024,2560]{1,0:T(8,128)(2,1)}) fusion(f32[1024,2560]{1,0:T(8,128)} %fusion.69, f32[1024,2560]{1,0:T(8,128)} %fusion.70, bf16[960,2560]{1,0:T(8,128)(2,1)} %bitcast.491, bf16[1024,960]{0,1:T(8,128)(2,1)} %reshape.517), kind=kOutput, calls=%fused_computation.6 | convolution fusion | flops 5072486400 | bytes 43581440 | tf_op jit(solution)/shard_map/dot_general | solution.py:129
  438.4 9.8 convolution_convert_fusion.2
  448.1 7.3 fusion.71
  455.5 7.2 convolution_convert_fusion.1
  499.0 9.3 reshape.580
  508.4 9.6 convolution_convert_fusion
  518.0 7.1 constant_dynamic-slice_fusion.2
  549.7 36.3 %attend_back.3 = (f32[5,4,64,384]{3,2,1,0:T(8,128)S(1)}, f32[5,2048,64]{2,1,0:T(8,128)}, f32[5,2048,64]{2,1,0:T(8,128)}) custom-call(bf16[5,4,384,64]{3,2,1,0:T(8,128)(2,1)S(1)} %bitcast.440, bf16[5,4,64,384]{3,2,1,0:T(8,128)(2,1)S(1)} %copy-done.20, bf16[5,4,384,64]{3,2,1,0:T(8,128)(2,1)S(1)} %bitcast.442, bf16[5,4,64,384]{3,2,1,0:T(8,128)(2,1)S(1)} %copy-done.22, ...), custom_call_target="tpu_custom_call" | custom-call | flops 25165824000 | bytes 7864320 | tf_op jit(solution)/shard_map/attend_back/pallas_call | solution.py:252
  595.1 7.3 copy.502
  616.0 36.1 %attend_back.2 = (f32[5,4,64,384]{3,2,1,0:T(8,128)S(1)}, f32[5,2048,64]{2,1,0:T(8,128)}, f32[5,2048,64]{2,1,0:T(8,128)}) custom-call(bf16[5,4,384,64]{3,2,1,0:T(8,128)(2,1)S(1)} %bitcast.439, bf16[5,4,64,384]{3,2,1,0:T(8,128)(2,1)S(1)} %copy-done.18, bf16[5,4,384,64]{3,2,1,0:T(8,128)(2,1)S(1)} %bitcast.441, bf16[5,4,64,384]{3,2,1,0:T(8,128)(2,1)S(1)} %copy-done.21, ...), custom_call_target="tpu_custom_call" | custom-call | flops 25165824000 | bytes 7864320 | tf_op jit(solution)/shard_map/attend_back/pallas_call | solution.py:252
  686.8 10.7 %fusion.21 = bf16[2,120,4,8,128]{4,3,2,1,0:T(8,128)(2,1)} fusion(f32[2,512,960]{1,2,0:T(8,128)} %copy-done.24, bf16[2,512,2560]{2,1,0:T(8,128)(2,1)} %bitcast.533, bf16[960,2560,1]{1,0,2:T(8,128)(2,1)} %reshape.580), kind=kOutput, calls=%fused_computation.70 | convolution fusion | flops 5035130880 | bytes 16056320 | tf_op jit(solution)/shard_map/dot_general | solution.py:48
  741.5 17.0 %collective-permute-done.1 = bf16[2,120,960]{2,1,0:T(8,128)(2,1)S(1)} collective-permute-done((bf16[2,120,960]{2,1,0:T(8,128)(2,1)S(1)}, bf16[2,120,960]{2,1,0:T(8,128)(2,1)S(1)}, u32[]{:S(2)}, u32[]{:S(2)}) %collective-permute-start.1) | collective-permute-done | bytes 460832 | tf_op jit(solution)/shard_map/ppermute | solution.py:59
  770.6 11.6 %collective-permute-done.13 = bf16[120,960]{0,1:T(8,128)(2,1)S(1)} collective-permute-done((bf16[120,960]{0,1:T(8,128)(2,1)S(1)}, bf16[120,960]{0,1:T(8,128)(2,1)S(1)}, u32[]{:S(2)}, u32[]{:S(2)}) %collective-permute-start.13) | collective-permute-done | bytes 230432 | tf_op jit(solution)/shard_map/ppermute | solution.py:59
  783.2 10.6 %collective-permute-done.3 = bf16[120,960]{1,0:T(8,128)(2,1)S(1)} collective-permute-done((bf16[120,960]{1,0:T(8,128)(2,1)S(1)}, bf16[120,960]{1,0:T(8,128)(2,1)S(1)}, u32[]{:S(2)}, u32[]{:S(2)}) %collective-permute-start.3) | collective-permute-done | bytes 230432 | tf_op jit(solution)/shard_map/ppermute | solution.py:59
  794.0 9.1 collective-permute-done.14
  821.0 20.1 %collective-permute-done.26 = bf16[2,120,2560]{2,1,0:T(8,128)(2,1)S(1)} collective-permute-done((bf16[2,120,2560]{2,1,0:T(8,128)(2,1)S(1)}, bf16[2,120,2560]{2,1,0:T(8,128)(2,1)S(1)}, u32[]{:S(2)}, u32[]{:S(2)}) %collective-permute-start.26) | collective-permute-done | bytes 1228832 | tf_op jit(solution)/shard_map/ppermute | solution.py:59
  842.9 23.5 %collective-permute-done.21 = bf16[2,120,2560]{2,1,0:T(8,128)(2,1)S(1)} collective-permute-done((bf16[2,120,2560]{2,1,0:T(8,128)(2,1)S(1)}, bf16[2,120,2560]{2,1,0:T(8,128)(2,1)S(1)}, u32[]{:S(2)}, u32[]{:S(2)}) %collective-permute-start.21) | collective-permute-done | bytes 1228832 | tf_op jit(solution)/shard_map/ppermute | solution.py:59
  875.0 7.8 collective-permute-done.22
  892.4 10.7 %collective-permute-done.23 = bf16[2,120,640]{2,1,0:T(8,128)(2,1)} collective-permute-done((bf16[2,120,640]{2,1,0:T(8,128)(2,1)}, bf16[2,120,640]{2,1,0:T(8,128)(2,1)}, u32[]{:S(2)}, u32[]{:S(2)}) %collective-permute-start.23) | collective-permute-done | bytes 307232 | tf_op jit(solution)/shard_map/ppermute | solution.py:59
  908.7 6.9 collective-permute-done.24
  944.2 23.7 %collective-permute-done.7 = bf16[120,640]{1,0:T(8,128)(2,1)S(1)} collective-permute-done((bf16[120,640]{1,0:T(8,128)(2,1)S(1)}, bf16[120,640]{1,0:T(8,128)(2,1)S(1)}, u32[]{:S(2)}, u32[]{:S(2)}) %collective-permute-start.7) | collective-permute-done | bytes 153632 | tf_op jit(solution)/shard_map/ppermute | solution.py:59
  968.0 39.8 %psum.7 = f32[2,960]{1,0:T(2,128)S(1)} all-reduce(f32[2,960]{1,0:T(2,128)S(1)} %pad_maximum_fusion.8), channel_id=1, replica_groups=mesh['fsdp'=2,'context'=4,'tensor'=4] {'fsdp','context','tensor'}, use_global_device_ids=true, to_apply=%region_8.9 | all-reduce | flops 1920 | bytes 15360 | tf_op jit(solution)/shard_map/psum | solution.py:449
  1008.6 7.9 collective-permute-done.9
  (453 shorter events, 491.1 us)
Async XLA Ops:
  7.2 61.2 %all-gather.6.cloned.1.call-start = ((), (), s32[]{:S(2)}) async-start(), calls=%async_computation.6 | async-start | bytes 5806080 | tf_op jit(solution)/shard_map/all_gather | solution.py:296
  17.5 40.1 %all-to-all-start = ((bf16[4,2,128,960]{2,1,3,0:T(2,128)(2,1)}), bf16[4,2,128,960]{2,1,3,0:T(2,128)(2,1)S(1)}, u32[]{:S(2)}, u32[]{:S(2)}) async-start(bf16[4,2,128,960]{2,1,3,0:T(2,128)(2,1)} %copy.454), calls=%async_computation | async-start | bytes 3932160 | tf_op jit(solution)/shard_map/all_to_all | solution.py:116
  21.7 171.3 %all-gather.8.cloned.1.call-start = ((), (), s32[]{:S(2)}) async-start(), calls=%async_computation.7 | async-start | bytes 3276800 | tf_op jit(solution)/shard_map/all_gather | solution.py:350
  101.2 155.1 %all-gather.10.cloned.1.call-start = ((), (), s32[]{:S(2)}) async-start(), calls=%async_computation.8 | async-start | bytes 3276800 | tf_op jit(solution)/shard_map/all_gather | solution.py:350
  102.9 257.4 %all-gather.12.cloned.1.call-start = ((), (), s32[]{:S(2)}) async-start(), calls=%async_computation.11 | async-start | bytes 15206400 | tf_op jit(solution)/shard_map/all_gather | solution.py:299
  110.2 28.8 %all-to-all-start.2 = ((bf16[4,2,128,960]{2,1,3,0:T(2,128)(2,1)}), bf16[4,2,128,960]{2,1,3,0:T(2,128)(2,1)}, u32[]{:S(2)}, u32[]{:S(2)}) async-start(bf16[4,2,128,960]{2,1,3,0:T(2,128)(2,1)} %copy.481), calls=%async_computation.2 | async-start | bytes 3932160 | tf_op jit(solution)/shard_map/all_to_all | solution.py:116
  114.6 801.8 %reduce-scatter.5.cloned.1.call-start = ((), (), s32[]{:S(2)}) async-start(), calls=%async_computation.10 | async-start | bytes 3276800 | tf_op jit(solution)/shard_map/reduce_scatter | solution.py:425
  526.8 282.0 %collective-permute-start.25 = (bf16[2,2,120,2560]{3,2,0,1:T(8,128)(2,1)}, bf16[2,2,120,2560]{3,2,0,1:T(8,128)(2,1)}, u32[]{:S(2)}, u32[]{:S(2)}) collective-permute-start(bf16[2,2,120,2560]{3,2,0,1:T(8,128)(2,1)} %bitcast.425), channel_id=1, source_target_pairs={{0,4},{4,0},{8,12},{12,8},{1,5},{5,1},{9,13},{13,9},{2,6},{6,2},{1... | collective-permute-start | bytes 7372808 | tf_op jit(solution)/shard_map/ppermute | solution.py:59
  528.4 284.8 %collective-permute-start.20 = (bf16[2,2,120,2560]{3,2,0,1:T(8,128)(2,1)}, bf16[2,2,120,2560]{3,2,0,1:T(8,128)(2,1)}, u32[]{:S(2)}, u32[]{:S(2)}) collective-permute-start(bf16[2,2,120,2560]{3,2,0,1:T(8,128)(2,1)} %bitcast.426), channel_id=1, source_target_pairs={{0,4},{4,0},{8,12},{12,8},{1,5},{5,1},{9,13},{13,9},{2,6},{6,2},{1... | collective-permute-start | bytes 7372808 | tf_op jit(solution)/shard_map/ppermute | solution.py:59
  532.2 285.0 %collective-permute-start.15 = (bf16[2,2,120,2560]{3,2,1,0:T(8,128)(2,1)}, bf16[2,2,120,2560]{3,2,1,0:T(8,128)(2,1)}, u32[]{:S(2)}, u32[]{:S(2)}) collective-permute-start(bf16[2,2,120,2560]{3,2,1,0:T(8,128)(2,1)} %dynamic-slice_bitcast_fusion), channel_id=1, source_target_pairs={{0,4},{4,0},{8,12},{12,8},{1,5},{5,1},{9,13},{13,9},{2,6},{6,2},{1... | collective-permute-start | bytes 7372808 | tf_op jit(solution)/shard_map/ppermute | solution.py:59
  685.2 38.6 %collective-permute-start.10 = (bf16[2,2,120,960]{2,3,1,0:T(8,128)(2,1)}, bf16[2,2,120,960]{2,3,1,0:T(8,128)(2,1)}, u32[]{:S(2)}, u32[]{:S(2)}) collective-permute-start(bf16[2,2,120,960]{2,3,1,0:T(8,128)(2,1)} %bitcast.87), channel_id=1, source_target_pairs={{0,4},{4,0},{8,12},{12,8},{1,5},{5,1},{9,13},{13,9},{2,6},{6,2},{1... | collective-permute-start | bytes 2764808 | tf_op jit(solution)/shard_map/ppermute | solution.py:59
  686.8 41.0 %collective-permute-start = (bf16[2,2,120,960]{3,2,0,1:T(8,128)(2,1)}, bf16[2,2,120,960]{3,2,0,1:T(8,128)(2,1)}, u32[]{:S(2)}, u32[]{:S(2)}) collective-permute-start(bf16[2,2,120,960]{3,2,0,1:T(8,128)(2,1)} %bitcast.433), channel_id=1, source_target_pairs={{0,4},{4,0},{8,12},{12,8},{1,5},{5,1},{9,13},{13,9},{2,6},{6,2},{1... | collective-permute-start | bytes 2764808 | tf_op jit(solution)/shard_map/ppermute | solution.py:59
  719.5 42.3 %all-to-all-start.1 = ((bf16[4,2,128,960]{2,3,1,0:T(8,128)(2,1)}), bf16[4,2,128,960]{2,3,1,0:T(8,128)(2,1)S(1)}, u32[]{:S(2)}, u32[]{:S(2)}) async-start(bf16[4,2,128,960]{2,3,1,0:T(8,128)(2,1)} %bitcast.463), calls=%async_computation.1 | async-start | bytes 3932160 | tf_op jit(solution)/shard_map/all_to_all | solution.py:124
  723.2 193.2 %reduce-scatter.3.cloned.1.call-start = ((), (), s32[]{:S(2)}) async-start(), calls=%async_computation.9 | async-start | bytes 3276800 | tf_op jit(solution)/shard_map/reduce_scatter | solution.py:425
  729.4 29.1 %collective-permute-start.1 = (bf16[2,120,960]{2,1,0:T(8,128)(2,1)S(1)}, bf16[2,120,960]{2,1,0:T(8,128)(2,1)S(1)}, u32[]{:S(2)}, u32[]{:S(2)}) collective-permute-start(bf16[2,120,960]{2,1,0:T(8,128)(2,1)S(1)} %dynamic-slice_bitcast_fusion.9), channel_id=1, source_target_pairs={{0,8},{4,12},{8,0},{12,4},{1,9},{5,13},{9,1},{13,5},{2,10},{6,14},... | collective-permute-start | bytes 1382408 | tf_op jit(solution)/shard_map/ppermute | solution.py:59
  739.8 24.3 %collective-permute-start.12 = (bf16[120,960]{0,1:T(8,128)(2,1)S(1)}, bf16[120,960]{0,1:T(8,128)(2,1)}, u32[]{:S(2)}, u32[]{:S(2)}) collective-permute-start(bf16[120,960]{0,1:T(8,128)(2,1)S(1)} %dynamic-slice_bitcast_fusion.14), channel_id=1, source_target_pairs={{0,8},{4,12},{8,0},{12,4},{1,9},{5,13},{9,1},{13,5},{2,10},{6,14},... | collective-permute-start | bytes 691208 | tf_op jit(solution)/shard_map/ppermute | solution.py:59
  765.3 16.9 %collective-permute-start.13 = (bf16[120,960]{0,1:T(8,128)(2,1)S(1)}, bf16[120,960]{0,1:T(8,128)(2,1)S(1)}, u32[]{:S(2)}, u32[]{:S(2)}) collective-permute-start(bf16[120,960]{0,1:T(8,128)(2,1)S(1)} %fusion.56), channel_id=1, source_target_pairs={{0,1},{1,0},{2,3},{3,2},{4,5},{5,4},{6,7},{7,6},{8,9},{9,8},{10,11... | collective-permute-start | bytes 691208 | tf_op jit(solution)/shard_map/ppermute | solution.py:59
  768.6 25.3 %collective-permute-start.3 = (bf16[120,960]{1,0:T(8,128)(2,1)S(1)}, bf16[120,960]{1,0:T(8,128)(2,1)S(1)}, u32[]{:S(2)}, u32[]{:S(2)}) collective-permute-start(bf16[120,960]{1,0:T(8,128)(2,1)S(1)} %fusion.57), channel_id=1, source_target_pairs={{0,1},{1,0},{2,3},{3,2},{4,5},{5,4},{6,7},{7,6},{8,9},{9,8},{10,11... | collective-permute-start | bytes 691208 | tf_op jit(solution)/shard_map/ppermute | solution.py:59
  782.3 20.9 %collective-permute-start.14 = (bf16[120,960]{0,1:T(8,128)(2,1)S(1)}, bf16[120,960]{0,1:T(8,128)(2,1)S(1)}, u32[]{:S(2)}, u32[]{:S(2)}) collective-permute-start(bf16[120,960]{0,1:T(8,128)(2,1)S(1)} %add_convert_fusion.2), channel_id=1, source_target_pairs={{0,2},{1,3},{2,0},{3,1},{4,6},{5,7},{6,4},{7,5},{8,10},{9,11},{10,... | collective-permute-start | bytes 691208 | tf_op jit(solution)/shard_map/ppermute | solution.py:59
  811.2 30.0 %collective-permute-start.26 = (bf16[2,120,2560]{2,1,0:T(8,128)(2,1)S(1)}, bf16[2,120,2560]{2,1,0:T(8,128)(2,1)S(1)}, u32[]{:S(2)}, u32[]{:S(2)}) collective-permute-start(bf16[2,120,2560]{2,1,0:T(8,128)(2,1)S(1)} %dynamic-slice_bitcast_fusion.1), channel_id=1, source_target_pairs={{0,8},{4,12},{8,0},{12,4},{1,9},{5,13},{9,1},{13,5},{2,10},{6,14},... | collective-permute-start | bytes 3686408 | tf_op jit(solution)/shard_map/ppermute | solution.py:59
  815.6 50.8 %collective-permute-start.21 = (bf16[2,120,2560]{2,1,0:T(8,128)(2,1)S(1)}, bf16[2,120,2560]{2,1,0:T(8,128)(2,1)S(1)}, u32[]{:S(2)}, u32[]{:S(2)}) collective-permute-start(bf16[2,120,2560]{2,1,0:T(8,128)(2,1)S(1)} %dynamic-slice_bitcast_fusion.2), channel_id=1, source_target_pairs={{0,8},{4,12},{8,0},{12,4},{1,9},{5,13},{9,1},{13,5},{2,10},{6,14},... | collective-permute-start | bytes 3686408 | tf_op jit(solution)/shard_map/ppermute | solution.py:59
  819.6 49.4 %collective-permute-start.16 = (bf16[2,120,2560]{2,1,0:T(8,128)(2,1)S(1)}, bf16[2,120,2560]{2,1,0:T(8,128)(2,1)S(1)}, u32[]{:S(2)}, u32[]{:S(2)}) collective-permute-start(bf16[2,120,2560]{2,1,0:T(8,128)(2,1)S(1)} %dynamic-slice_bitcast_fusion.3), channel_id=1, source_target_pairs={{0,16},{16,0},{1,17},{17,1},{2,18},{18,2},{3,19},{19,3},{4,20},{20... | collective-permute-start | bytes 3686408 | tf_op jit(solution)/shard_map/ppermute | solution.py:59
  841.5 30.4 %collective-permute-start.27 = (bf16[120,2560]{1,0:T(8,128)(2,1)S(1)}, bf16[120,2560]{1,0:T(8,128)(2,1)S(1)}, u32[]{:S(2)}, u32[]{:S(2)}) collective-permute-start(bf16[120,2560]{1,0:T(8,128)(2,1)S(1)} %dynamic-slice_bitcast_fusion.4), channel_id=1, source_target_pairs={{0,16},{16,0},{1,17},{17,1},{2,18},{18,2},{3,19},{19,3},{4,20},{20... | collective-permute-start | bytes 1843208 | tf_op jit(solution)/shard_map/ppermute | solution.py:59
  870.2 17.5 %collective-permute-start.17 = (bf16[120,2560]{1,0:T(8,128)(2,1)}, bf16[120,2560]{1,0:T(8,128)(2,1)}, u32[]{:S(2)}, u32[]{:S(2)}) collective-permute-start(bf16[120,2560]{1,0:T(8,128)(2,1)} %dynamic-slice_bitcast_fusion.6), channel_id=1, source_target_pairs={{0,8},{4,12},{8,0},{12,4},{1,9},{5,13},{9,1},{13,5},{2,10},{6,14},... | collective-permute-start | bytes 1843208 | tf_op jit(solution)/shard_map/ppermute | solution.py:59
  875.0 16.2 %collective-permute-start.28 = (bf16[2,120,640]{2,1,0:T(8,128)(2,1)}, bf16[2,120,640]{2,1,0:T(8,128)(2,1)}, u32[]{:S(2)}, u32[]{:S(2)}) collective-permute-start(bf16[2,120,640]{2,1,0:T(8,128)(2,1)} %dynamic-slice_bitcast_fusion.10), channel_id=1, source_target_pairs={{0,1},{1,0},{2,3},{3,2},{4,5},{5,4},{6,7},{7,6},{8,9},{9,8},{10,11... | collective-permute-start | bytes 921608 | tf_op jit(solution)/shard_map/ppermute | solution.py:59
  887.7 15.5 %collective-permute-start.23 = (bf16[2,120,640]{2,1,0:T(8,128)(2,1)}, bf16[2,120,640]{2,1,0:T(8,128)(2,1)}, u32[]{:S(2)}, u32[]{:S(2)}) collective-permute-start(bf16[2,120,640]{2,1,0:T(8,128)(2,1)} %dynamic-slice_bitcast_fusion.11), channel_id=1, source_target_pairs={{0,1},{1,0},{2,3},{3,2},{4,5},{5,4},{6,7},{7,6},{8,9},{9,8},{10,11... | collective-permute-start | bytes 921608 | tf_op jit(solution)/shard_map/ppermute | solution.py:59
  889.2 17.6 %collective-permute-start.18 = (bf16[2,120,640]{2,1,0:T(8,128)(2,1)S(1)}, bf16[2,120,640]{2,1,0:T(8,128)(2,1)S(1)}, u32[]{:S(2)}, u32[]{:S(2)}) collective-permute-start(bf16[2,120,640]{2,1,0:T(8,128)(2,1)S(1)} %dynamic-slice_bitcast_fusion.12), channel_id=1, source_target_pairs={{0,1},{1,0},{2,3},{3,2},{4,5},{5,4},{6,7},{7,6},{8,9},{9,8},{10,11... | collective-permute-start | bytes 921608 | tf_op jit(solution)/shard_map/ppermute | solution.py:59
  892.3 15.7 %collective-permute-start.29 = (bf16[1,120,640]{2,1,0:T(8,128)(2,1)S(1)}, bf16[1,120,640]{2,1,0:T(8,128)(2,1)S(1)}, u32[]{:S(2)}, u32[]{:S(2)}) collective-permute-start(bf16[1,120,640]{2,1,0:T(8,128)(2,1)S(1)} %constant_dynamic-slice_fusion), channel_id=1, source_target_pairs={{0,2},{1,3},{2,0},{3,1},{4,6},{5,7},{6,4},{7,5},{8,10},{9,11},{10,... | collective-permute-start | bytes 460808 | tf_op jit(solution)/shard_map/ppermute | solution.py:59
  907.5 35.0 %collective-permute-start.19 = (bf16[1,120,640]{2,1,0:T(8,128)(2,1)}, bf16[1,120,640]{2,1,0:T(8,128)(2,1)}, u32[]{:S(2)}, u32[]{:S(2)}) collective-permute-start(bf16[1,120,640]{2,1,0:T(8,128)(2,1)} %constant_dynamic-slice_fusion.6), channel_id=1, source_target_pairs={{0,2},{1,3},{2,0},{3,1},{4,6},{5,7},{6,4},{7,5},{8,10},{9,11},{10,... | collective-permute-start | bytes 460808 | tf_op jit(solution)/shard_map/ppermute | solution.py:59
  936.6 81.7 %all-to-all-start.3 = ((bf16[4,2,128,960]{2,3,1,0:T(8,128)(2,1)}), bf16[4,2,128,960]{2,3,1,0:T(8,128)(2,1)S(1)}, u32[]{:S(2)}, u32[]{:S(2)}) async-start(bf16[4,2,128,960]{2,3,1,0:T(8,128)(2,1)} %bitcast_bitcast_fusion), calls=%async_computation.5 | async-start | bytes 3932160 | tf_op jit(solution)/shard_map/all_to_all | solution.py:124
  940.5 27.4 %collective-permute-start.7 = (bf16[120,640]{1,0:T(8,128)(2,1)S(1)}, bf16[120,640]{1,0:T(8,128)(2,1)S(1)}, u32[]{:S(2)}, u32[]{:S(2)}) collective-permute-start(bf16[120,640]{1,0:T(8,128)(2,1)S(1)} %dynamic-slice_bitcast_fusion.16), channel_id=1, source_target_pairs={{0,8},{4,12},{8,0},{12,4},{1,9},{5,13},{9,1},{13,5},{2,10},{6,14},... | collective-permute-start | bytes 460808 | tf_op jit(solution)/shard_map/ppermute | solution.py:59
  967.9 40.0 %collective-permute-start.8 = (bf16[120,640]{1,0:T(8,128)(2,1)S(1)}, bf16[120,640]{1,0:T(8,128)(2,1)S(1)}, u32[]{:S(2)}, u32[]{:S(2)}) collective-permute-start(bf16[120,640]{1,0:T(8,128)(2,1)S(1)} %fusion.58), channel_id=1, source_target_pairs={{0,1},{1,0},{2,3},{3,2},{4,5},{5,4},{6,7},{7,6},{8,9},{9,8},{10,11... | collective-permute-start | bytes 460808 | tf_op jit(solution)/shard_map/ppermute | solution.py:59
  (88 other events, 731.9 us)
Sparse Core Ops, SparseCore 0:
  14.3 53.9 all-gather.5
  101.3 55.9 all-gather.7
  158.8 53.5 all-gather.9
  215.7 104.7 all-gather.11
  607.7 53.1 reduce-scatter.4
  726.1 63.4 reduce-scatter.2
